TPU v7x, 32 devices: a whole 2x2x4 slice. The times are simulated.
32 devices in a mesh: rep: 1, ep: 8 (over z, y), dp: 2 (over x), sp: 2 (over core).
Axes of the slice: x: 2, y: 2, z: 4, core: 2. Of those that a mesh axis runs over, the one named last changes fastest.
Arguments:
- hidden_states: bfloat16 [2048, 4096], P(('rep', 'ep', 'sp'), 'dp'), may hold values from -6 to 6
- norm_gain: bfloat16 [4096], P('dp'), may hold values from 0.099609375 to 1.8984375
- up_proj: bfloat16 [16, 4096, 768], P(('ep', 'sp'), 'dp'), may hold values from -0.09375 to 0.09375
- down_proj: bfloat16 [16, 768, 4096], P(('ep', 'sp'), None, 'dp'), may hold values from -0.21875 to 0.21875
- expert_ids: int32 [2048, 8], P(('rep', 'ep', 'sp')), may hold values from 0 to 15, all different within a row; in each aligned block of 128 rows (0 to 127, 128 to 255, ...) at most 80 rows name the same one
- combine_num: int32 [2048, 8], P(('rep', 'ep', 'sp')), may hold values from 2048 to 65535
Outputs:
- mixed: bfloat16 [2048, 4096], P(('rep', 'ep', 'sp'), 'dp')
Inputs may be any that keep to these rules, and one draw needn't show every extreme that they name: `expert_ids`: each row names 8 different experts; among the 128 rows that one device holds (an aligned block) no expert is named more than 80 times, a bound that some block reaches.
All inputs are finite; a program needn't handle non-finite values.
Results may differ from a plain program's by a relative error of at most 0.008.
Values may be sent and summed in bfloat16 or wider, within the bound.
A program may use at most 64 MiB of HBM per device.

v0:
```python
import jax
import jax.numpy as jnp
from jax import lax
from jax.sharding import PartitionSpec as P

D = 4096


def body(hidden_states, norm_gain, up_proj, down_proj, expert_ids, combine_num):
    token_count, local_width = hidden_states.shape
    top_count = expert_ids.shape[1]
    ep_count = lax.axis_size("ep")
    sp_count = lax.axis_size("sp")
    expert_count = ep_count * sp_count
    routed = token_count * top_count
    capacity = max(2, min(token_count, routed // expert_count + routed // (4 * expert_count)))
    slot_count = expert_count * capacity
    widened = hidden_states.astype(jnp.float32)
    square_part = jnp.sum(widened * widened, axis=-1)
    square_total = lax.psum(square_part, "dp")
    mean_sq = (square_total / D)[:, None]
    normed = (widened * lax.rsqrt(mean_sq + 1e-06) * norm_gain.astype(jnp.float32)).astype(
        jnp.bfloat16
    )
    flat_expert = expert_ids.reshape(-1)
    onehot = (flat_expert[:, None] == jnp.arange(expert_count, dtype=jnp.int32)[None, :]).astype(
        jnp.int32
    )
    before = jnp.cumsum(onehot, axis=0) - onehot
    position = jnp.sum(before * onehot, axis=1)
    target = flat_expert * capacity + position
    placed = (jnp.arange(slot_count, dtype=jnp.int32)[:, None] == target[None, :]).astype(
        jnp.float32
    )
    select = placed.reshape(slot_count, token_count, top_count).sum(axis=2)
    outgoing = jnp.dot(select.astype(jnp.bfloat16), normed, preferred_element_type=jnp.float32)
    outgoing = outgoing.astype(jnp.bfloat16).reshape(expert_count, capacity, local_width)
    weights = combine_num.reshape(-1).astype(jnp.float32) / 65536.0
    mixing = (placed * weights[None, :]).reshape(slot_count, token_count, top_count).sum(axis=2)
    mixing_high = mixing.astype(jnp.bfloat16)
    mixing_low = (mixing - mixing_high.astype(jnp.float32)).astype(jnp.bfloat16)
    incoming = lax.all_to_all(outgoing, ("ep", "sp"), split_axis=0, concat_axis=0, tiled=True)
    arriving = incoming.reshape(slot_count, local_width)
    up_local = up_proj[0]
    down_local = down_proj[0]
    partial_value = jnp.dot(arriving, up_local, preferred_element_type=jnp.float32)
    summed = lax.psum(partial_value, "dp")
    hidden = jax.nn.silu(summed).astype(jnp.bfloat16)
    produced = jnp.dot(hidden, down_local, preferred_element_type=jnp.float32).astype(jnp.bfloat16)
    leaving = produced.reshape(expert_count, capacity, local_width)
    returned = lax.all_to_all(leaving, ("ep", "sp"), split_axis=0, concat_axis=0, tiled=True)
    back_rows = returned.reshape(slot_count, local_width)
    mixed = jnp.einsum("st,sd->td", mixing_high, back_rows, preferred_element_type=jnp.float32)
    mixed = mixed + jnp.einsum(
        "st,sd->td", mixing_low, back_rows, preferred_element_type=jnp.float32
    )
    return mixed.astype(jnp.bfloat16)


def solution(mesh):
    placed = (
        P(("rep", "ep", "sp"), "dp"),
        P("dp"),
        P(("ep", "sp"), "dp", None),
        P(("ep", "sp"), None, "dp"),
        P(("rep", "ep", "sp"), None),
        P(("rep", "ep", "sp"), None),
    )
    return jax.shard_map(
        body, mesh=mesh, in_specs=placed, out_specs=P(("rep", "ep", "sp"), "dp"), check_vma=False
    )
```

profile of v0, /device:TPU:0, one launch (start us, length us, event | category | flops | bytes accessed | tf_op | source)
XLA Modules:
  0.0 399.0 jit_solution(11997309658928762221)
XLA Ops:
  6.5 0.0 copy-start
  6.5 0.0 all-reduce.2.cloned.1.call-start
  6.5 0.9 copy.25
  7.5 0.1 eq.45
  7.6 0.1 eq.41
  7.7 1.2 fusion.5
  8.9 5.8 %psum.14 = f32[128]{0:T(128)S(1)} all-reduce(f32[128]{0:T(128)S(1)} %fusion.5), channel_id=1, replica_groups=mesh['rep'=1,'ep'=8,'dp'=2,'sp'=2] {'dp'}, use_global_device_ids=true, to_apply=%region_6.7 | all-reduce | flops 128 | bytes 1024 | tf_op jit(solution)/shard_map/psum | solution.py:20
  14.7 0.7 convert_multiply_fusion.2
  15.4 0.7 convert_element_type.58
  16.1 4.5 %reduce-window.6 = s32[16,8,128]{2,1,0:T(8,128)S(1)} reduce-window(s32[16,8,128]{2,1,0:T(8,128)S(1)} %fusion.18, s32[]{:T(128)} %constant.16.clone.1), window={size=1x1x128 pad=0_0x0_0x127_0}, to_apply=%region_0.0 | reduce-window | flops 2080768 | bytes 131076 | tf_op jit(solution)/shard_map/reduce-window
  20.6 0.1 slice.8
  20.7 0.1 copy.27
  20.9 0.1 copy.28
  21.0 0.1 broadcast_add_fusion
  21.1 0.1 reduce_sum.39
  21.2 0.7 multiply_add_fusion
  21.9 6.8 %select_reduce_fusion = (f32[1280,128]{1,0:T(8,128)}, bf16[1280,128]{1,0:T(8,128)(2,1)S(1)}) fusion(f32[128,8]{0,1:T(8,128)S(1)} %convert_multiply_fusion.2, s32[128,8]{0,1:T(8,128)S(1)} %multiply_add_fusion), kind=kLoop, calls=%fused_computation.3 | loop fusion | flops 6225920 | bytes 991232 | tf_op jit(solution)/shard_map/reduce_sum | solution.py:39
  28.7 2.7 convolution_convert_fusion.1
  31.4 0.0 copy-start.2
  31.4 121.3 %all_to_all.10 = bf16[16,80,2048]{2,1,0:T(8,128)(2,1)S(1)} all-to-all(bf16[16,80,2048]{2,1,0:T(8,128)(2,1)S(1)} %bitcast.34), channel_id=1, replica_groups=mesh['rep'=1,'ep'=8,'dp'=2,'sp'=2] {'ep','sp'}, dimensions={0} | all-to-all | bytes 10485760 | tf_op jit(solution)/shard_map/all_to_all | solution.py:42
  152.7 0.0 copy-done.2
  152.7 6.2 %fusion.1 = f32[1280,768]{1,0:T(8,128)} fusion(bf16[1280,2048]{1,0:T(8,128)(2,1)S(1)} %bitcast.35, bf16[1,2048,768]{2,1,0:T(8,128)(2,1)S(1)} %copy-done.2), kind=kOutput, calls=%fused_computation.7 | convolution fusion | flops 4026531840 | bytes 12320768 | tf_op jit(solution)/shard_map/dot_general | solution.py:46
  158.8 0.0 all-reduce.2.cloned.1.call-update
  158.9 103.8 %all-reduce.2.cloned.1.call-done = f32[1280,768]{1,0:T(8,128)} async-done(((f32[1280,768]{1,0:T(8,128)}), f32[1280,768]{1,0:T(8,128)}) %all-reduce.2.cloned.1.call-update) | async-done | bytes 3932176 | tf_op jit(solution)/shard_map/psum | solution.py:47
  262.6 0.0 copy-done
  262.6 6.6 %convolution_convert_fusion = bf16[1280,2048]{1,0:T(8,128)(2,1)S(1)} fusion(bf16[1,768,2048]{2,1,0:T(8,128)(2,1)S(1)} %copy-done, f32[1280,768]{1,0:T(8,128)} %all-reduce.2.cloned.1.call-done), kind=kOutput, calls=%fused_computation | convolution fusion | flops 4034068480 | bytes 12320768 | tf_op jit(solution)/shard_map/dot_general | solution.py:49
  269.3 0.0 copy-start.1
  269.3 120.3 %all_to_all.11 = bf16[16,80,2048]{2,1,0:T(8,128)(2,1)S(1)} all-to-all(bf16[16,80,2048]{2,1,0:T(8,128)(2,1)S(1)} %bitcast.36), channel_id=1, replica_groups=mesh['rep'=1,'ep'=8,'dp'=2,'sp'=2] {'ep','sp'}, dimensions={0} | all-to-all | bytes 10485760 | tf_op jit(solution)/shard_map/all_to_all | solution.py:51
  389.6 0.0 copy-done.1
  389.6 0.9 fusion.13
  390.5 1.7 fusion.3
  (6 shorter events, 0.1 us)
Async XLA Ops:
  6.5 256.1 %copy-start = (bf16[1,768,2048]{2,1,0:T(8,128)(2,1)S(1)}, bf16[1,768,2048]{2,1,0:T(8,128)(2,1)}, u32[]{:S(2)}) copy-start(bf16[1,768,2048]{2,1,0:T(8,128)(2,1)} %param.9) | copy-start | bytes 9437188
  6.5 256.1 %all-reduce.2.cloned.1.call-start = ((), (), s32[]{:S(2)}) async-start(), calls=%async_computation.2 | async-start | bytes 7864320 | tf_op jit(solution)/shard_map/psum | solution.py:47
  31.4 121.3 %copy-start.2 = (bf16[1,2048,768]{2,1,0:T(8,128)(2,1)S(1)}, bf16[1,2048,768]{2,1,0:T(8,128)(2,1)}, u32[]{:S(2)}) copy-start(bf16[1,2048,768]{2,1,0:T(8,128)(2,1)} %param.8) | copy-start | bytes 9437188
  269.3 120.3 %copy-start.1 = (f32[1280,128]{1,0:T(8,128)S(1)}, f32[1280,128]{1,0:T(8,128)}, u32[]{:S(2)}) copy-start(f32[1280,128]{1,0:T(8,128)} %get-tuple-element.5) | copy-start | bytes 1966084
Sparse Core Ops, SparseCore 0:
  159.0 103.5 all-reduce.1
where the time goes:
time: 400 us; the launch traced here: 399 us
  blocking collectives  247 us (62%)
  waiting for transfers between devices  104 us (26%)
  matrix products  18 us (4%)
  other arithmetic  14.8 us (4%)
  between operations  13.5 us (3%)
    all_to_all x1, blocking collectives, body(): lax.all_to_all(outgoing, ('ep', 'sp'), split_axis=0, concat_axis=0, tiled...  121 us
    all_to_all x1, blocking collectives, body(): lax.all_to_all(leaving, ('ep', 'sp'), split_axis=0, concat_axis=0, tiled=...  120 us
    psum x1, waiting for transfers between devices, body(): summed = lax.psum(partial_value, 'dp')  104 us
  transfers between devices with their start and end apart: 1, of which 1 were waited for; matrix products, arithmetic and copies ran while one was open for 0% of the time, Pallas kernels for 0%

commit v1 on v0

v1 whole, which is shorter than its diff:
```python
import functools

import jax
import jax.numpy as jnp
from jax import lax
from jax.experimental import pallas as pl
from jax.experimental.pallas import tpu as pltpu
from jax.sharding import PartitionSpec as P

D = 4096
EPS = 1e-06
YS = 2
F32 = jnp.float32
BF16 = jnp.bfloat16


def routed_body(hidden_states, norm_gain, up_proj, down_proj, expert_ids, combine_num):
    token_count, local_width = hidden_states.shape
    top_count = expert_ids.shape[1]
    ep_count = lax.axis_size("ep")
    sp_count = lax.axis_size("sp")
    expert_count = ep_count * sp_count
    routed = token_count * top_count
    capacity = max(2, min(token_count, routed // expert_count + routed // (4 * expert_count)))
    slot_count = expert_count * capacity
    widened = hidden_states.astype(F32)
    square_part = jnp.sum(widened * widened, axis=-1)
    square_total = lax.psum(square_part, "dp")
    mean_sq = (square_total / D)[:, None]
    normed = (widened * lax.rsqrt(mean_sq + EPS) * norm_gain.astype(F32)).astype(BF16)
    flat_expert = expert_ids.reshape(-1)
    onehot = (flat_expert[:, None] == jnp.arange(expert_count, dtype=jnp.int32)[None, :]).astype(
        jnp.int32
    )
    before = jnp.cumsum(onehot, axis=0) - onehot
    position = jnp.sum(before * onehot, axis=1)
    target = flat_expert * capacity + position
    placed = (jnp.arange(slot_count, dtype=jnp.int32)[:, None] == target[None, :]).astype(F32)
    select = placed.reshape(slot_count, token_count, top_count).sum(axis=2)
    outgoing = jnp.dot(select.astype(BF16), normed, preferred_element_type=F32)
    outgoing = outgoing.astype(BF16).reshape(expert_count, capacity, local_width)
    weights = combine_num.reshape(-1).astype(F32) / 65536.0
    mixing = (placed * weights[None, :]).reshape(slot_count, token_count, top_count).sum(axis=2)
    mixing_high = mixing.astype(BF16)
    mixing_low = (mixing - mixing_high.astype(F32)).astype(BF16)
    incoming = lax.all_to_all(outgoing, ("ep", "sp"), split_axis=0, concat_axis=0, tiled=True)
    arriving = incoming.reshape(slot_count, local_width)
    partial_value = jnp.dot(arriving, up_proj[0], preferred_element_type=F32)
    summed = lax.psum(partial_value, "dp")
    hidden = jax.nn.silu(summed).astype(BF16)
    produced = jnp.dot(hidden, down_proj[0], preferred_element_type=F32).astype(BF16)
    leaving = produced.reshape(expert_count, capacity, local_width)
    returned = lax.all_to_all(leaving, ("ep", "sp"), split_axis=0, concat_axis=0, tiled=True)
    back_rows = returned.reshape(slot_count, local_width)
    mixed = jnp.einsum("st,sd->td", mixing_high, back_rows, preferred_element_type=F32)
    mixed = mixed + jnp.einsum("st,sd->td", mixing_low, back_rows, preferred_element_type=F32)
    return mixed.astype(BF16)


def kernel(cap, nz, h_hbm, g_ref, u_hbm, d_hbm, ids_ref, num_ref, out_ref,
           xg, sg, u_ref, d_ref, cbuf, pown, psend, precv, sqs, sqp, w8, rk8, selb, wcol, rcol,
           hid, yb, crecv, yrecv, zb, za,
           lsem, agr, su, sd, sy, sc, ss, sr, xs, xr, qs, qr, cs, cr, ys, yr, zs_s, zbr, zar):
    toks, width = h_hbm.shape
    ff = u_hbm.shape[2]
    top = ids_ref.shape[1]
    ep, c, x = lax.axis_index("ep"), lax.axis_index("sp"), lax.axis_index("dp")
    z, y = lax.div(ep, YS), lax.rem(ep, YS)
    me, oth = y * 2 + c, (1 - y) * 2 + c
    mec, othc = y * 2 + 1 - c, (1 - y) * 2 + 1 - c
    expert = ep * 2 + c
    up_dev, dn_dev = {"ep": ep + YS}, {"ep": ep - YS}
    y_dev, c_dev, x_dev = {"ep": ep + 1 - 2 * y}, {"sp": 1 - c}, {"dp": 1 - x}

    def rc(src, dst, ssem, rsem, dev):
        return pltpu.make_async_remote_copy(
            src_ref=src, dst_ref=dst, send_sem=ssem, recv_sem=rsem,
            device_id=dev, device_id_type=pl.DeviceIdType.MESH)

    def z_dev(d):
        return {"ep": lax.rem(z + d, nz) * YS + y}

    load_h = pltpu.make_async_copy(h_hbm, xg.at[z, me], lsem.at[0])
    load_u = pltpu.make_async_copy(u_hbm.at[0], u_ref, lsem.at[1])
    load_d = pltpu.make_async_copy(d_hbm.at[0], d_ref, lsem.at[2])
    load_h.start()
    load_u.start()
    load_d.start()

    barrier = pltpu.get_barrier_semaphore()
    partners = [y_dev, c_dev, x_dev] + [z_dev(d) for d in range(1, nz)]
    for dev in partners:
        pl.semaphore_signal(barrier, inc=1, device_id=dev, device_id_type=pl.DeviceIdType.MESH)
    pl.semaphore_wait(barrier, len(partners))

    def z_up(zs):
        return rc(xg.at[zs, me], xg.at[zs, me], su.at[zs], agr.at[zs, me], up_dev)

    def z_dn(zs):
        return rc(xg.at[zs, me], xg.at[zs, me], sd.at[zs], agr.at[zs, me], dn_dev)

    def to_y(zs):
        return rc(xg.at[zs, me], xg.at[zs, me], sy.at[zs], agr.at[zs, me], y_dev)

    def to_c(zs, which):
        slot = me if which == 0 else oth
        return rc(xg.at[zs, slot], xg.at[zs, slot], sc.at[zs, which], agr.at[zs, slot], c_dev)

    def arrived(zs, slot):
        rc(xg.at[zs, slot], xg.at[zs, slot], sc.at[zs, 0], agr.at[zs, slot], c_dev).wait_recv()

    load_h.wait()

    @pl.when(z < nz - 1)
    def _():
        z_up(z).start()

    @pl.when(z > 0)
    def _():
        z_dn(z).start()

    lane = lax.broadcasted_iota(jnp.int32, (toks, 128), 1)
    hv = xg[z, me].astype(F32)
    acc = jnp.where(lane == 16, jnp.sum(hv * hv, axis=1, keepdims=True), 0.0)
    for k in range(top):
        wk = num_ref[:, k:k + 1].astype(F32) * (1.0 / 65536.0)
        acc = acc + jnp.where(lane == ids_ref[:, k:k + 1], wk, 0.0)
    sg[z, me] = acc.T[:24]
    st_c = rc(sg.at[z, me], sg.at[z, me], ss.at[0], sr.at[nz], c_dev)
    st_c.start()
    to_c(z, 0).start()
    st_c.wait_recv()
    pair = pl.ds(y * 2, 2)
    st_y = rc(sg.at[z, pair], sg.at[z, pair], ss.at[1], sr.at[nz + 1], y_dev)
    st_y.start()
    to_y(z).start()
    st_y.wait_recv()
    st_z = [rc(sg.at[z], sg.at[z], ss.at[1 + d], sr.at[z], z_dev(d)) for d in range(1, nz)]
    for cp in st_z:
        cp.start()

    def hop(h):
        @pl.when(z >= h)
        def _():
            zs = z - h
            arrived(zs, me)

            @pl.when(z < nz - 1)
            def _():
                z_up(zs).start()
            to_y(zs).start()
            to_c(zs, 0).start()

        @pl.when(z + h < nz)
        def _():
            zs = z + h
            arrived(zs, me)

            @pl.when(z > 0)
            def _():
                z_dn(zs).start()
            to_y(zs).start()
            to_c(zs, 0).start()

    low = z < 2
    order = [z, z + 1 - 2 * lax.rem(z, 2), jnp.where(low, 2, 1), jnp.where(low, 3, 0)]
    tri = (lax.broadcasted_iota(jnp.int32, (toks, toks), 0)
           < lax.broadcasted_iota(jnp.int32, (toks, toks), 1)).astype(BF16)
    spot = lax.broadcasted_iota(jnp.int32, (cap, toks), 0)

    def x_copy(k):
        return rc(psend.at[k], precv.at[k], xs.at[k], xr.at[k], x_dev)

    def q_copy(k):
        return rc(sqs.at[k], sqp.at[k], qs.at[k], qr.at[k], x_dev)

    def first(k):
        zs = order[k]
        if k > 0:
            rc(sg.at[zs], sg.at[zs], ss.at[2], sr.at[zs], c_dev).wait_recv()
        for s in range(4):
            w8[k, s:s + 1] = sg[zs, s, pl.ds(expert, 1), :]
            sqs[k, s:s + 1] = sg[zs, s, 16:17, :]
            w8[k, 4 + s:5 + s] = jnp.zeros((1, toks), F32)
            sqs[k, 4 + s:5 + s] = jnp.zeros((1, toks), F32)
        q_copy(k).start()
        named = w8[k] > 0.0
        rank = jnp.dot(named.astype(F32).astype(BF16), tri, preferred_element_type=F32)
        rk8[k] = jnp.where(named, rank.astype(jnp.int32), -1)
        for s in range(4):
            sel = spot == rk8[k, s:s + 1]
            selb[k, s * cap:(s + 1) * cap] = sel.astype(F32).astype(BF16)
            wcol[k, s * cap:(s + 1) * cap] = jnp.sum(
                jnp.where(sel, w8[k, s:s + 1], 0.0), axis=1, keepdims=True)
        arrived(zs, oth)
        to_c(zs, 1).start()
        arrived(zs, mec)
        arrived(zs, othc)

        @pl.loop(0, width // 512)
        def _(t):
            cols = pl.ds(pl.multiple_of(t * 512, 512), 512)
            gain = g_ref[:, cols].astype(F32)
            for s in range(4):
                rows = slice(s * cap, (s + 1) * cap)
                picked = jnp.dot(selb[k, rows], xg[zs, s, :, cols], preferred_element_type=F32)
                cbuf[rows, cols] = (picked * gain).astype(BF16)

        if k == 0:
            load_u.wait()

        @pl.loop(0, ff // 256)
        def _(t):
            cols = pl.ds(pl.multiple_of(t * 256, 256), 256)
            part = jnp.dot(cbuf[...], u_ref[:, cols], preferred_element_type=F32)
            pown[k, :, cols] = part
            psend[k, :, cols] = part.astype(BF16)
        x_copy(k).start()

    for k in range(nz):
        if k < nz - 1:
            hop(k + 1)
        first(k)

    def core_copy(k, yy):
        return rc(yb.at[k, yy * 2 + 1 - c], crecv.at[k, yy], cs.at[k, yy], cr.at[k, yy], c_dev)

    def core_arrived(k, yy):
        rc(yb.at[k, me], crecv.at[k, yy], cs.at[k, 0], cr.at[k, yy], c_dev).wait_recv()

    def y_copy(k):
        return rc(yb.at[k, oth], yrecv.at[k], ys.at[k], yr.at[k], y_dev)

    def up_copy(k, zs):
        return rc(yb.at[k, me], zb.at[zs], zs_s.at[k], zbr.at[zs], up_dev)

    def dn_copy(k, zs):
        return rc(yb.at[k, me], za.at[zs], zs_s.at[k], zar.at[zs], dn_dev)

    def second(k):
        q_copy(k).wait_recv()
        scale = lax.rsqrt((sqs[k] + sqp[k]) * (1.0 / D) + EPS)
        for s in range(4):
            sel = spot == rk8[k, s:s + 1]
            rcol[s * cap:(s + 1) * cap] = jnp.sum(
                jnp.where(sel, scale[s:s + 1], 0.0), axis=1, keepdims=True)
        x_copy(k).wait_recv()

        @pl.loop(0, ff // 256)
        def _(t):
            cols = pl.ds(pl.multiple_of(t * 256, 256), 256)
            v = (pown[k, :, cols] + precv[k, :, cols].astype(F32)) * rcol[...]
            hid[:, cols] = (v / (1.0 + jnp.exp(-v))).astype(BF16)

        @pl.loop(0, width // 512)
        def _(t):
            cols = pl.ds(pl.multiple_of(t * 512, 512), 512)
            made = jnp.dot(hid[...], d_ref[:, cols], preferred_element_type=F32)
            made = (made * wcol[k]).astype(BF16)
            for s in range(4):
                rows = slice(s * cap, (s + 1) * cap)
                yb[k, s, :, cols] = lax.dot_general(
                    selb[k, rows], made[rows], (((0,), (0,)), ((), ())),
                    preferred_element_type=F32).astype(BF16)
        core_copy(k, 1 - y).start()
        core_copy(k, y).start()

    def across(k):
        core_arrived(k, 1 - y)
        yb[k, oth] = (yb[k, oth].astype(F32) + crecv[k, 1 - y].astype(F32)).astype(BF16)
        y_copy(k).start()

    def along(k):
        zs = order[k]
        core_arrived(k, y)
        y_copy(k).wait_recv()
        total = yb[k, me].astype(F32) + crecv[k, y].astype(F32) + yrecv[k].astype(F32)
        if k == 0:
            out_ref[...] = total.astype(BF16)

            @pl.when((z > 0) & (z < nz - 1))
            def _():
                up_copy(k, zs).wait_recv()
                dn_copy(k, zs).wait_recv()
                out_ref[...] = (total + zb[zs].astype(F32) + za[zs].astype(F32)).astype(BF16)

            @pl.when(z == 0)
            def _():
                dn_copy(k, zs).wait_recv()
                out_ref[...] = (total + za[zs].astype(F32)).astype(BF16)

            @pl.when(z == nz - 1)
            def _():
                up_copy(k, zs).wait_recv()
                out_ref[...] = (total + zb[zs].astype(F32)).astype(BF16)
        else:
            yb[k, me] = total.astype(BF16)

            @pl.when((zs > z) & (z > 0))
            def _():
                up_copy(k, zs).wait_recv()
                yb[k, me] = (total + zb[zs].astype(F32)).astype(BF16)

            @pl.when((zs < z) & (z < nz - 1))
            def _():
                dn_copy(k, zs).wait_recv()
                yb[k, me] = (total + za[zs].astype(F32)).astype(BF16)

            @pl.when(zs > z)
            def _():
                up_copy(k, zs).start()

            @pl.when(zs < z)
            def _():
                dn_copy(k, zs).start()

    load_d.wait()
    second(2)
    across(2)
    second(3)
    across(3)
    along(2)
    second(1)
    across(1)
    along(3)
    second(0)
    across(0)
    along(1)
    along(0)

    for zs in range(nz):
        @pl.when((zs <= z) & (z < nz - 1))
        def _():
            z_up(zs).wait_send()

        @pl.when((zs >= z) & (z > 0))
        def _():
            z_dn(zs).wait_send()
        to_y(zs).wait_send()
        to_c(zs, 0).wait_send()
        to_c(zs, 1).wait_send()
    st_c.wait_send()
    st_y.wait_send()
    for cp in st_z:
        cp.wait_send()
    for k in range(nz):
        x_copy(k).wait_send()
        q_copy(k).wait_send()
        core_copy(k, y).wait_send()
        core_copy(k, 1 - y).wait_send()
        y_copy(k).wait_send()
        if k > 0:
            up_copy(k, order[k]).wait_send()


def dense_body(hidden_states, norm_gain, up_proj, down_proj, expert_ids, combine_num):
    toks, width = hidden_states.shape
    top = expert_ids.shape[1]
    ff = up_proj.shape[2]
    nz = lax.axis_size("ep") // YS
    experts = lax.axis_size("ep") * lax.axis_size("sp")
    routed = toks * top
    cap = min(toks, routed // experts + routed // (4 * experts))
    rows = 4 * cap
    dma = pltpu.SemaphoreType.DMA
    vmem = pl.BlockSpec(memory_space=pltpu.VMEM)
    hbm = pl.BlockSpec(memory_space=pl.ANY)
    return pl.pallas_call(
        functools.partial(kernel, cap, nz),
        out_shape=jax.ShapeDtypeStruct((toks, width), BF16),
        in_specs=[hbm, vmem, hbm, hbm, vmem, vmem],
        out_specs=vmem,
        scratch_shapes=[
            pltpu.VMEM((nz, 4, toks, width), BF16),
            pltpu.VMEM((nz, 4, 24, toks), F32),
            pltpu.VMEM((width, ff), BF16),
            pltpu.VMEM((ff, width), BF16),
            pltpu.VMEM((rows, width), BF16),
            pltpu.VMEM((nz, rows, ff), F32),
            pltpu.VMEM((nz, rows, ff), BF16),
            pltpu.VMEM((nz, rows, ff), BF16),
            pltpu.VMEM((nz, 8, toks), F32),
            pltpu.VMEM((nz, 8, toks), F32),
            pltpu.VMEM((nz, 8, toks), F32),
            pltpu.VMEM((nz, 8, toks), jnp.int32),
            pltpu.VMEM((nz, rows, toks), BF16),
            pltpu.VMEM((nz, rows, 1), F32),
            pltpu.VMEM((rows, 1), F32),
            pltpu.VMEM((rows, ff), BF16),
            pltpu.VMEM((nz, 4, toks, width), BF16),
            pltpu.VMEM((nz, 2, toks, width), BF16),
            pltpu.VMEM((nz, toks, width), BF16),
            pltpu.VMEM((nz, toks, width), BF16),
            pltpu.VMEM((nz, toks, width), BF16),
            dma((3,)), dma((nz, 4)), dma((nz,)), dma((nz,)), dma((nz,)), dma((nz, 2)),
            dma((nz + 1,)), dma((nz + 2,)), dma((nz,)), dma((nz,)), dma((nz,)), dma((nz,)),
            dma((nz, 2)), dma((nz, 2)), dma((nz,)), dma((nz,)), dma((nz,)), dma((nz,)), dma((nz,)),
        ],
        compiler_params=pltpu.CompilerParams(
            collective_id=0, has_side_effects=True, vmem_limit_bytes=58 * 1024 * 1024),
        cost_estimate=pl.CostEstimate(
            flops=4 * 4 * rows * width * ff, bytes_accessed=4 * width * ff, transcendentals=0),
    )(hidden_states, norm_gain.reshape(1, width), up_proj, down_proj, expert_ids, combine_num)


def solution(mesh):
    spec = (
        P(("rep", "ep", "sp"), "dp"),
        P("dp"),
        P(("ep", "sp"), "dp", None),
        P(("ep", "sp"), None, "dp"),
        P(("rep", "ep", "sp"), None),
        P(("rep", "ep", "sp"), None),
    )
    sizes = dict(mesh.shape)
    dense = (sizes["rep"], sizes["ep"], sizes["dp"], sizes["sp"]) == (1, 8, 2, 2)
    return jax.shard_map(
        dense_body if dense else routed_body,
        mesh=mesh, in_specs=spec, out_specs=P(("rep", "ep", "sp"), "dp"), check_vma=False
    )
```

time: 400 us -> 132 us (0.33)
  blocking collectives: 247 us -> 0 us
  Pallas kernels: 0 us -> 125 us
  waiting for transfers between devices: 104 us -> 0 us
  matrix products: 18 us -> 0 us
  other arithmetic: 14.8 us -> 0 us
  between operations: 13.5 us -> 0.01 us
  local copies, waits for them, and re-layouts: 1.54 us -> 5.99 us
    all_to_all x2 -> x0, blocking collectives: 242 us -> none  [the longest x1 121 us: body(): lax.all_to_all(outgoing, ('ep', 'sp'), split_axis=0, concat_axis=0, tiled...]
    pallas_call x0 -> x1, Pallas kernels: none -> 125 us  [dense_body(): pl.pallas_call(functools.partial(kernel, cap, nz), out_shape=jax.ShapeDty...]
    psum x1 -> x0, waiting for transfers between devices: 104 us -> none  [body(): summed = lax.psum(partial_value, 'dp')]
    dot_general x5 -> x0, matrix products: 18 us -> none  [the longest x1 6.65 us: body(): jnp.dot(hidden, down_local, preferred_element_type=jnp.float32)]
    reduce_sum x3 -> x0, other arithmetic: 8.05 us -> none  [the longest x1 6.79 us: body(): (placed * weights[None, :]).reshape(slot_count, token_count, top_count)]
    psum x1 -> x0, blocking collectives: 5.83 us -> none  [body(): square_total = lax.psum(square_part, 'dp')]
    another operation x3 -> x0, other arithmetic: 4.64 us -> none
  transfers between devices with their start and end apart: 1 -> 0, of which waited for: 1 -> 0; matrix products, arithmetic and copies ran while one was open for 0% -> 0% of each run, Pallas kernels for 0% -> 0%
where the time goes in v1:
time: 132 us; the launch traced here: 131 us
  Pallas kernels  125 us (95%)
  local copies, waits for them, and re-layouts  5.99 us (5%)
    pallas_call x1, Pallas kernels, dense_body(): pl.pallas_call(functools.partial(kernel, cap, nz), out_shape=jax.ShapeDty...  125 us
    unnamed x3, local copies, waits for them, and re-layouts  4.7 us

profile of v1, /device:TPU:0, one launch (start us, length us, event | category | flops | bytes accessed | tf_op | source)
XLA Modules:
  0.0 131.3 jit_solution(5891084641586904759)
XLA Ops:
  0.0 1.3 reshape.3.g_ref
  1.3 1.4 %copy.7.ids_ref = s32[128,8]{1,0:T(8,128)} copy(s32[128,8]{0,1:T(8,128)} %param.10) | data formatting | bytes 8192 | tf_op args[4]
  2.7 1.4 %copy.8.num_ref = s32[128,8]{1,0:T(8,128)} copy(s32[128,8]{0,1:T(8,128)} %param.11) | data formatting | bytes 8192 | tf_op args[5]
  4.1 125.3 %shard_map.64 = bf16[128,2048]{1,0:T(8,128)(2,1)} custom-call(bf16[128,2048]{1,0:T(8,128)(2,1)} %h_hbm.1, bf16[1,2048]{1,0:T(2,128)(2,1)} %reshape.3.g_ref, bf16[1,2048,768]{2,1,0:T(8,128)(2,1)} %u_hbm.1, bf16[1,768,2048]{2,1,0:T(8,128)(2,1)} %d_hbm.1, s32[128,8]{1,0:T(8,128)} %copy.7.ids_ref, s32[128,8]{1,0:T(8,128)} %copy.8.num_ref), custom_call_target="tpu_custom_call" | custom-call | flops 8053063680 | bytes 6291456 | tf_op jit(solution)/shard_map/pallas_call | solution.py:368
  129.4 1.9 %copy.10 = bf16[128,2048]{1,0:T(8,128)(2,1)} copy(bf16[128,2048]{1,0:T(8,128)(2,1)} %shard_map.64) | data formatting | bytes 1048576

commit v2 on v1

v2 whole, which is shorter than its diff:
```python
import functools

import jax
import jax.numpy as jnp
from jax import lax
from jax.experimental import pallas as pl
from jax.experimental.pallas import tpu as pltpu
from jax.sharding import PartitionSpec as P

D = 4096
EPS = 1e-06
IN_PARTS = 2
BACK_PARTS = 4
YS = 2
F32 = jnp.float32
BF16 = jnp.bfloat16


def routed_body(hidden_states, norm_gain, up_proj, down_proj, expert_ids, combine_num):
    token_count, local_width = hidden_states.shape
    top_count = expert_ids.shape[1]
    ep_count = lax.axis_size("ep")
    sp_count = lax.axis_size("sp")
    expert_count = ep_count * sp_count
    routed = token_count * top_count
    capacity = max(2, min(token_count, routed // expert_count + routed // (4 * expert_count)))
    slot_count = expert_count * capacity
    widened = hidden_states.astype(F32)
    square_part = jnp.sum(widened * widened, axis=-1)
    square_total = lax.psum(square_part, "dp")
    mean_sq = (square_total / D)[:, None]
    normed = (widened * lax.rsqrt(mean_sq + EPS) * norm_gain.astype(F32)).astype(BF16)
    flat_expert = expert_ids.reshape(-1)
    onehot = (flat_expert[:, None] == jnp.arange(expert_count, dtype=jnp.int32)[None, :]).astype(
        jnp.int32
    )
    before = jnp.cumsum(onehot, axis=0) - onehot
    position = jnp.sum(before * onehot, axis=1)
    target = flat_expert * capacity + position
    placed = (jnp.arange(slot_count, dtype=jnp.int32)[:, None] == target[None, :]).astype(F32)
    select = placed.reshape(slot_count, token_count, top_count).sum(axis=2)
    outgoing = jnp.dot(select.astype(BF16), normed, preferred_element_type=F32)
    outgoing = outgoing.astype(BF16).reshape(expert_count, capacity, local_width)
    weights = combine_num.reshape(-1).astype(F32) / 65536.0
    mixing = (placed * weights[None, :]).reshape(slot_count, token_count, top_count).sum(axis=2)
    mixing_high = mixing.astype(BF16)
    mixing_low = (mixing - mixing_high.astype(F32)).astype(BF16)
    incoming = lax.all_to_all(outgoing, ("ep", "sp"), split_axis=0, concat_axis=0, tiled=True)
    arriving = incoming.reshape(slot_count, local_width)
    partial_value = jnp.dot(arriving, up_proj[0], preferred_element_type=F32)
    summed = lax.psum(partial_value, "dp")
    hidden = jax.nn.silu(summed).astype(BF16)
    produced = jnp.dot(hidden, down_proj[0], preferred_element_type=F32).astype(BF16)
    leaving = produced.reshape(expert_count, capacity, local_width)
    returned = lax.all_to_all(leaving, ("ep", "sp"), split_axis=0, concat_axis=0, tiled=True)
    back_rows = returned.reshape(slot_count, local_width)
    mixed = jnp.einsum("st,sd->td", mixing_high, back_rows, preferred_element_type=F32)
    mixed = mixed + jnp.einsum("st,sd->td", mixing_low, back_rows, preferred_element_type=F32)
    return mixed.astype(BF16)


def kernel(cap, nz, h_hbm, g_ref, u_hbm, d_hbm, ids_ref, num_ref, out_ref,
           xg, sg, u_ref, d_ref, cbuf, pown, psend, precv, sqs, sqp, w8, rk8, selb, wcol, rcol,
           hid, yb, crecv, yrecv, zb, za, gs,
           lsem, agr, su, sd, sy, sc, ss, sr, xs, xr, qs, qr, cs, cr, ys, yr, zs_s, zbr, zar):
    toks, width = h_hbm.shape
    ff = u_hbm.shape[2]
    top = ids_ref.shape[0]
    step_in, step_back = width // IN_PARTS, width // BACK_PARTS
    parts_in = [pl.ds(i * step_in, step_in) for i in range(IN_PARTS)]
    parts_back = [pl.ds(i * step_back, step_back) for i in range(BACK_PARTS)]
    ep, c, x = lax.axis_index("ep"), lax.axis_index("sp"), lax.axis_index("dp")
    z, y = lax.div(ep, YS), lax.rem(ep, YS)
    me, oth = y * 2 + c, (1 - y) * 2 + c
    mec, othc = y * 2 + 1 - c, (1 - y) * 2 + 1 - c
    expert = ep * 2 + c
    up_dev, dn_dev = {"ep": ep + YS}, {"ep": ep - YS}
    y_dev, c_dev, x_dev = {"ep": ep + 1 - 2 * y}, {"sp": 1 - c}, {"dp": 1 - x}

    def rc(src, dst, ssem, rsem, dev):
        return pltpu.make_async_remote_copy(
            src_ref=src, dst_ref=dst, send_sem=ssem, recv_sem=rsem,
            device_id=dev, device_id_type=pl.DeviceIdType.MESH)

    def z_dev(d):
        return {"ep": lax.rem(z + d, nz) * YS + y}

    load_h = pltpu.make_async_copy(h_hbm, xg.at[z, me], lsem.at[0])
    load_u = pltpu.make_async_copy(u_hbm.at[0], u_ref, lsem.at[1])
    load_d = pltpu.make_async_copy(d_hbm.at[0], d_ref, lsem.at[2])
    load_h.start()
    load_u.start()
    load_d.start()

    barrier = pltpu.get_barrier_semaphore()
    partners = [y_dev, c_dev, x_dev] + [z_dev(d) for d in range(1, nz)]
    for dev in partners:
        pl.semaphore_signal(barrier, inc=1, device_id=dev, device_id_type=pl.DeviceIdType.MESH)
    pl.semaphore_wait(barrier, len(partners))

    def z_up(zs, i):
        ref = xg.at[zs, me, :, parts_in[i]]
        return rc(ref, ref, su.at[zs, i], agr.at[zs, me, i], up_dev)

    def z_dn(zs, i):
        ref = xg.at[zs, me, :, parts_in[i]]
        return rc(ref, ref, sd.at[zs, i], agr.at[zs, me, i], dn_dev)

    def to_y(zs, i):
        ref = xg.at[zs, me, :, parts_in[i]]
        return rc(ref, ref, sy.at[zs, i], agr.at[zs, me, i], y_dev)

    def from_y(zs, i):
        ref = xg.at[zs, oth, :, parts_in[i]]
        rc(ref, ref, sy.at[zs, i], agr.at[zs, oth, i], y_dev).wait_recv()

    def to_c(zs, which):
        slot = me if which == 0 else oth
        return rc(xg.at[zs, slot], xg.at[zs, slot], sc.at[zs, which], agr.at[zs, slot, 0], c_dev)

    def arrived(zs, slot):
        rc(xg.at[zs, slot], xg.at[zs, slot], sc.at[zs, 0], agr.at[zs, slot, 0], c_dev).wait_recv()

    load_h.wait()

    for i in range(IN_PARTS):
        @pl.when(z < nz - 1)
        def _():
            z_up(z, i).start()

        @pl.when(z > 0)
        def _():
            z_dn(z, i).start()

    row = lax.broadcasted_iota(jnp.int32, (24, toks), 0)
    hv = xg[z, me].astype(F32)
    squares = jnp.broadcast_to(jnp.sum(hv * hv, axis=1, keepdims=True), (toks, 128)).T
    acc = jnp.where(row == 16, squares[:24], 0.0)
    for k in range(top):
        wk = num_ref[k:k + 1].astype(F32) * (1.0 / 65536.0)
        acc = acc + jnp.where(row == ids_ref[k:k + 1], wk, 0.0)
    sg[z, me] = acc
    st_c = rc(sg.at[z, me], sg.at[z, me], ss.at[0], sr.at[nz], c_dev)
    st_c.start()
    to_c(z, 0).start()
    st_c.wait_recv()
    pair = pl.ds(y * 2, 2)
    st_y = rc(sg.at[z, pair], sg.at[z, pair], ss.at[1], sr.at[nz + 1], y_dev)
    st_y.start()
    for i in range(IN_PARTS):
        to_y(z, i).start()
    st_y.wait_recv()
    st_z = [rc(sg.at[z], sg.at[z], ss.at[1 + d], sr.at[z], z_dev(d)) for d in range(1, nz)]
    for cp in st_z:
        cp.start()

    def hop(h):
        for i in range(IN_PARTS):
            @pl.when(z >= h)
            def _():
                z_up(z - h, i).wait_recv()

                @pl.when(z < nz - 1)
                def _():
                    z_up(z - h, i).start()
                to_y(z - h, i).start()

            @pl.when(z + h < nz)
            def _():
                z_dn(z + h, i).wait_recv()

                @pl.when(z > 0)
                def _():
                    z_dn(z + h, i).start()
                to_y(z + h, i).start()

        @pl.when(z >= h)
        def _():
            to_c(z - h, 0).start()

        @pl.when(z + h < nz)
        def _():
            to_c(z + h, 0).start()

    gs[...] = g_ref[...].astype(F32).reshape(1, width)
    inner = (z > 0) & (z < nz - 1)
    order = [z, 1 + lax.rem(z, 2),
             jnp.where(z == 0, 2, jnp.where(z == 1, 0, jnp.where(z == 2, 3, 1))),
             jnp.where(z < 2, 3, 0)]
    tri = (lax.broadcasted_iota(jnp.int32, (toks, toks), 0)
           < lax.broadcasted_iota(jnp.int32, (toks, toks), 1)).astype(BF16)
    spot = lax.broadcasted_iota(jnp.int32, (cap, toks), 0)

    def half_rows(yy):
        return pl.ds(pl.multiple_of(yy * 2 * cap, 16), 2 * cap)

    def x_copy(k, yy):
        rows = half_rows(yy)
        return rc(psend.at[k, rows], precv.at[k, rows], xs.at[k, yy], xr.at[k, yy], x_dev)

    def q_copy(k):
        return rc(sqs.at[k], sqp.at[k], qs.at[k], qr.at[k], x_dev)

    def first(k):
        zs = order[k]
        if k > 0:
            rc(sg.at[zs], sg.at[zs], ss.at[2], sr.at[zs], c_dev).wait_recv()
        for s in range(4):
            w8[k, s:s + 1] = sg[zs, s, pl.ds(expert, 1), :]
            sqs[k, s:s + 1] = sg[zs, s, 16:17, :]
            w8[k, 4 + s:5 + s] = jnp.zeros((1, toks), F32)
            sqs[k, 4 + s:5 + s] = jnp.zeros((1, toks), F32)
        q_copy(k).start()
        named = w8[k] > 0.0
        rank = jnp.dot(named.astype(F32).astype(BF16), tri, preferred_element_type=F32)
        rk8[k] = jnp.where(named, rank.astype(jnp.int32), -1)
        for s in range(4):
            sel = spot == rk8[k, s:s + 1]
            selb[k, s * cap:(s + 1) * cap] = sel.astype(F32).astype(BF16)
            wcol[k, s * cap:(s + 1) * cap] = jnp.sum(
                jnp.where(sel, w8[k, s:s + 1], 0.0), axis=1, keepdims=True)
        arrived(zs, mec)
        up_half(k, zs, y)
        for i in range(IN_PARTS):
            from_y(zs, i)
        to_c(zs, 1).start()
        arrived(zs, othc)
        up_half(k, zs, 1 - y)

    def up_half(k, zs, yy):
        @pl.loop(0, width // 512)
        def _(t):
            cols = pl.ds(pl.multiple_of(t * 512, 512), 512)
            for j in range(2):
                s = yy * 2 + j
                rows = pl.ds(pl.multiple_of(s * cap, 16), cap)
                picked = jnp.dot(selb[k, rows], xg[zs, s, :, cols], preferred_element_type=F32)
                cbuf[j * cap:(j + 1) * cap, cols] = (picked * gs[:, cols]).astype(BF16)

        half = half_rows(yy)

        @pl.loop(0, ff // 256)
        def _(t):
            cols = pl.ds(pl.multiple_of(t * 256, 256), 256)
            part = jnp.dot(cbuf[...], u_ref[:, cols], preferred_element_type=F32)
            pown[k, half, cols] = part
            psend[k, half, cols] = part.astype(BF16)
        x_copy(k, yy).start()

    load_u.wait()
    def core_copy(k, yy, i):
        cols = parts_back[i]
        return rc(yb.at[k, yy * 2 + 1 - c, :, cols], crecv.at[k, yy, :, cols],
                  cs.at[k, yy, i], cr.at[k, yy, i], c_dev)

    def y_copy(k, i):
        cols = parts_back[i]
        return rc(yb.at[k, oth, :, cols], yrecv.at[k, :, cols], ys.at[k, i], yr.at[k, i], y_dev)

    def up_copy(k, zs, i):
        cols = parts_back[i]
        return rc(yb.at[k, me, :, cols], zb.at[zs, :, cols], zs_s.at[k, i], zbr.at[zs, i], up_dev)

    def dn_copy(k, zs, i):
        cols = parts_back[i]
        return rc(yb.at[k, me, :, cols], za.at[zs, :, cols], zs_s.at[k, i], zar.at[zs, i], dn_dev)

    def second(k):
        q_copy(k).wait_recv()
        scale = lax.rsqrt((sqs[k] + sqp[k]) * (1.0 / D) + EPS)
        for s in range(4):
            sel = spot == rk8[k, s:s + 1]
            rcol[s * cap:(s + 1) * cap] = jnp.sum(
                jnp.where(sel, scale[s:s + 1], 0.0), axis=1, keepdims=True)
        x_copy(k, y).wait_recv()
        x_copy(k, 1 - y).wait_recv()

        @pl.loop(0, ff // 256)
        def _(t):
            cols = pl.ds(pl.multiple_of(t * 256, 256), 256)
            v = (pown[k, :, cols] + precv[k, :, cols].astype(F32)) * rcol[...]
            hid[:, cols] = (v / (1.0 + jnp.exp(-v))).astype(BF16)

        def produce(cols):
            made = jnp.dot(hid[...], d_ref[:, cols], preferred_element_type=F32)
            made = (made * wcol[k]).astype(BF16)
            for s in range(4):
                rows = slice(s * cap, (s + 1) * cap)
                yb[k, s, :, cols] = lax.dot_general(
                    selb[k, rows], made[rows], (((0,), (0,)), ((), ())),
                    preferred_element_type=F32).astype(BF16)

        for i in range(BACK_PARTS):
            @pl.loop(0, step_back // 512)
            def _(t):
                produce(pl.ds(pl.multiple_of(i * step_back + t * 512, 512), 512))
            core_copy(k, 1 - y, i).start()
            core_copy(k, y, i).start()

    def across(k):
        for i, cols in enumerate(parts_back):
            core_copy(k, 1 - y, i).wait_recv()
            yb[k, oth, :, cols] = (yb[k, oth, :, cols].astype(F32)
                                   + crecv[k, 1 - y, :, cols].astype(F32)).astype(BF16)
            y_copy(k, i).start()

    def along(k, zs, last=False):
        for i, cols in enumerate(parts_back):
            core_copy(k, y, i).wait_recv()
            y_copy(k, i).wait_recv()

            def add(chains):
                total = (yb[k, me, :, cols].astype(F32) + crecv[k, y, :, cols].astype(F32)
                         + yrecv[k, :, cols].astype(F32))
                for copy, buf in chains:
                    copy(k, zs, i).wait_recv()
                    total = total + buf[zs, :, cols].astype(F32)
                if last:
                    out_ref[:, cols] = total.astype(BF16)
                else:
                    yb[k, me, :, cols] = total.astype(BF16)

            below, above = (up_copy, zb), (dn_copy, za)
            if last:
                pl.when(inner)(lambda: add([below, above]))
                pl.when(z == 0)(lambda: add([above]))
                pl.when(z == nz - 1)(lambda: add([below]))
            else:
                pl.when(inner & (zs > z))(lambda: add([below]))
                pl.when(inner & (zs < z))(lambda: add([above]))
                pl.when((z == 0) | (z == nz - 1))(lambda: add([]))

                @pl.when(zs > z)
                def _():
                    up_copy(k, zs, i).start()

                @pl.when(zs < z)
                def _():
                    dn_copy(k, zs, i).start()

    hop(1)
    first(0)
    hop(2)
    first(1)
    hop(3)
    first(2)
    load_d.wait()
    late = jnp.where(inner, 3, 2), jnp.where(inner, 2, 3)
    dest = jnp.where(inner, order[3], order[2]), jnp.where(inner, order[2], order[3])
    second(1)
    across(1)
    first(3)
    second(2)
    across(2)
    along(1, order[1])
    second(3)
    across(3)
    second(0)
    across(0)
    along(late[0], dest[0])
    along(late[1], dest[1])
    along(0, order[0], True)

    for zs in range(nz):
        for i in range(IN_PARTS):
            @pl.when((zs <= z) & (z < nz - 1))
            def _():
                z_up(zs, i).wait_send()

            @pl.when((zs >= z) & (z > 0))
            def _():
                z_dn(zs, i).wait_send()
            to_y(zs, i).wait_send()
        to_c(zs, 0).wait_send()
        to_c(zs, 1).wait_send()
    st_c.wait_send()
    st_y.wait_send()
    for cp in st_z:
        cp.wait_send()
    for k in range(nz):
        x_copy(k, y).wait_send()
        x_copy(k, 1 - y).wait_send()
        q_copy(k).wait_send()
        for i in range(BACK_PARTS):
            core_copy(k, y, i).wait_send()
            core_copy(k, 1 - y, i).wait_send()
            y_copy(k, i).wait_send()
            if k > 0:
                up_copy(k, order[k], i).wait_send()


def dense_body(hidden_states, norm_gain, up_proj, down_proj, expert_ids, combine_num):
    toks, width = hidden_states.shape
    top = expert_ids.shape[1]
    ff = up_proj.shape[2]
    nz = lax.axis_size("ep") // YS
    experts = lax.axis_size("ep") * lax.axis_size("sp")
    routed = toks * top
    cap = min(toks, routed // experts + routed // (4 * experts))
    rows = 4 * cap
    ni, nb = IN_PARTS, BACK_PARTS
    dma = pltpu.SemaphoreType.DMA
    vmem = pl.BlockSpec(memory_space=pltpu.VMEM)
    hbm = pl.BlockSpec(memory_space=pl.ANY)
    return pl.pallas_call(
        functools.partial(kernel, cap, nz),
        out_shape=jax.ShapeDtypeStruct((toks, width), BF16),
        in_specs=[hbm, vmem, hbm, hbm, vmem, vmem],
        out_specs=vmem,
        scratch_shapes=[
            pltpu.VMEM((nz, 4, toks, width), BF16),
            pltpu.VMEM((nz, 4, 24, toks), F32),
            pltpu.VMEM((width, ff), BF16),
            pltpu.VMEM((ff, width), BF16),
            pltpu.VMEM((2 * cap, width), BF16),
            pltpu.VMEM((nz, rows, ff), F32),
            pltpu.VMEM((nz, rows, ff), BF16),
            pltpu.VMEM((nz, rows, ff), BF16),
            pltpu.VMEM((nz, 8, toks), F32),
            pltpu.VMEM((nz, 8, toks), F32),
            pltpu.VMEM((nz, 8, toks), F32),
            pltpu.VMEM((nz, 8, toks), jnp.int32),
            pltpu.VMEM((nz, rows, toks), BF16),
            pltpu.VMEM((nz, rows, 1), F32),
            pltpu.VMEM((rows, 1), F32),
            pltpu.VMEM((rows, ff), BF16),
            pltpu.VMEM((nz, 4, toks, width), BF16),
            pltpu.VMEM((nz, 2, toks, width), BF16),
            pltpu.VMEM((nz, toks, width), BF16),
            pltpu.VMEM((nz, toks, width), BF16),
            pltpu.VMEM((nz, toks, width), BF16),
            pltpu.VMEM((1, width), F32),
            dma((3,)), dma((nz, 4, ni)), dma((nz, ni)), dma((nz, ni)), dma((nz, ni)), dma((nz, 2)),
            dma((nz + 1,)), dma((nz + 2,)), dma((nz, 2)), dma((nz, 2)), dma((nz,)), dma((nz,)),
            dma((nz, 2, nb)), dma((nz, 2, nb)), dma((nz, nb)), dma((nz, nb)), dma((nz, nb)),
            dma((nz, nb)), dma((nz, nb)),
        ],
        compiler_params=pltpu.CompilerParams(
            collective_id=0, has_side_effects=True, vmem_limit_bytes=58 * 1024 * 1024),
        cost_estimate=pl.CostEstimate(
            flops=4 * 4 * rows * width * ff, bytes_accessed=4 * width * ff, transcendentals=0),
    )(hidden_states, norm_gain, up_proj, down_proj, expert_ids.T, combine_num.T)


def solution(mesh):
    spec = (
        P(("rep", "ep", "sp"), "dp"),
        P("dp"),
        P(("ep", "sp"), "dp", None),
        P(("ep", "sp"), None, "dp"),
        P(("rep", "ep", "sp"), None),
        P(("rep", "ep", "sp"), None),
    )
    sizes = dict(mesh.shape)
    dense = (sizes["rep"], sizes["ep"], sizes["dp"], sizes["sp"]) == (1, 8, 2, 2)
    return jax.shard_map(
        dense_body if dense else routed_body,
        mesh=mesh, in_specs=spec, out_specs=P(("rep", "ep", "sp"), "dp"), check_vma=False
    )
```

time: 132 us -> 124 us (0.939)
  local copies, waits for them, and re-layouts: 5.99 us -> 1.88 us
  Pallas kernels: 125 us -> 122 us
    pallas_call x1, Pallas kernels: 125 us -> 122 us  [dense_body(): pl.pallas_call(functools.partial(kernel, cap, nz), out_shape=jax.ShapeDty...]
    unnamed x3 -> x1, local copies, waits for them, and re-layouts: 4.7 us -> 1.88 us
where the time goes in v2:
time: 124 us
  Pallas kernels  122 us (98%)
  local copies, waits for them, and re-layouts  1.88 us (2%)
    pallas_call x1, Pallas kernels, dense_body(): pl.pallas_call(functools.partial(kernel, cap, nz), out_shape=jax.ShapeDty...  122 us

profile of v2, /device:TPU:0, one launch (start us, length us, event | category | flops | bytes accessed | tf_op | source)
XLA Modules:
  0.0 124.3 jit_solution(9795186313351484143)
XLA Ops:
  0.0 122.4 %shard_map.64 = bf16[128,2048]{1,0:T(8,128)(2,1)} custom-call(bf16[128,2048]{1,0:T(8,128)(2,1)} %h_hbm.1, bf16[2048]{0:T(1024)(128)(2,1)} %g_ref.1, bf16[1,2048,768]{2,1,0:T(8,128)(2,1)} %u_hbm.1, bf16[1,768,2048]{2,1,0:T(8,128)(2,1)} %d_hbm.1, s32[8,128]{1,0:T(8,128)} %bitcast.2, s32[8,128]{1,0:T(8,128)} %bitcast.3), custom_call_target="tpu_custom_call" | custom-call | flops 8053063680 | bytes 6291456 | tf_op jit(solution)/shard_map/pallas_call | solution.py:405
  122.4 1.9 %copy.8 = bf16[128,2048]{1,0:T(8,128)(2,1)} copy(bf16[128,2048]{1,0:T(8,128)(2,1)} %shard_map.64) | data formatting | bytes 1048576
